TPU v7x, 256 devices: a whole 4x4x8 slice. The times are simulated.
256 devices in a mesh: node: 16 (over x, y), feat: 16 (over z, core).
Axes of the slice: x: 4, y: 4, z: 8, core: 2. Of those that a mesh axis runs over, the one named last changes fastest.
Arguments:
- feats_t: float32 [512, 16384], P('feat', 'node'), may hold values from -6 to 6
- weight: float32 [512, 512], P(None, 'feat'), may hold values from -0.25 to 0.25
- cot_t: float32 [512, 16384], P('feat', 'node'), may hold values from -6 to 6
- tiles: float32 [128, 8, 128, 128], P('node'), may hold values from -0.1875 to 0.1875
- col_ids: int32 [128, 8], P('node'), may hold values from 0 to 127, as said below
- counts: int32 [128], P('node'), may hold values from 1 to 8, as said below
Outputs:
- out_t: float32 [512, 16384], P('feat', 'node')
- grad_feats: float32 [512, 16384], P('feat', 'node')
- grad_weight: float32 [512, 512], P(None, 'feat')
Inputs may be any that keep to these rules, and one draw needn't show every extreme that they name: `col_ids`: column block c belongs to node index c // 8. Among the 64 slots of one node index's row blocks, at most 4 name column blocks of any one node index, and some node index is named by exactly 4; ids may repeat within a row block. `counts`: row block 0 has all 8 slots live; loads differ between devices.
All inputs are finite; a program needn't handle non-finite values.
Results may differ from a plain program's by a relative error of at most 0.0001.
Values sent between devices are 32-bit elements; how exact they have to be, the bound alone decides.
A program may use at most 64 MiB of HBM per device.

v0:
```python
import jax
import jax.numpy as jnp
from jax import lax
from jax.sharding import PartitionSpec as P

HIGH = lax.Precision.HIGHEST


def from_root(value, axis, source):
    kept = jnp.where(lax.axis_index(axis) == source, value, 0).astype(value.dtype)
    return lax.psum(kept, axis)


def on_device(feats_t, weight, cot_t, tiles, col_ids, counts):
    width_part, rows = feats_t.shape
    nblocks = tiles.shape[0]
    slots = tiles.shape[1]
    local_blocks = rows // 128
    node_count = lax.axis_size("node")
    total = local_blocks * node_count
    live = (jnp.arange(slots)[None, :] < counts[:, None]).astype(jnp.float32)
    empty = jnp.zeros((width_part, nblocks, slots, 128), jnp.float32)
    owner = col_ids // local_blocks
    within = col_ids % local_blocks

    def section(root, selected):
        received = from_root(feats_t, "node", root)
        shaped = received.reshape(width_part, local_blocks, 128)
        picked = jnp.take(shaped, within, axis=1)
        return jnp.where((owner == root)[None, :, :, None], picked, selected)

    selected = lax.fori_loop(0, node_count, section, empty)
    selected = selected * live[None, :, :, None]
    mixed_t = jnp.einsum("fbkc,bkrc->fbr", selected, tiles, precision=HIGH).reshape(
        width_part, rows
    )
    mixed_full = lax.all_gather(mixed_t, "feat", axis=0, tiled=True)
    pre_t = jnp.dot(weight.T, mixed_full, precision=HIGH)
    sig = jax.nn.sigmoid(pre_t)
    out_t = pre_t * sig
    grad_pre = cot_t * (sig * (1.0 + pre_t * (1.0 - sig)))
    grad_weight = lax.psum(jnp.dot(mixed_full, grad_pre.T, precision=HIGH), "node")
    grad_mixed = lax.psum_scatter(
        jnp.dot(weight, grad_pre, precision=HIGH), "feat", scatter_dimension=0, tiled=True
    )
    contrib = jnp.einsum(
        "fbr,bkrc->fbkc", grad_mixed.reshape(width_part, nblocks, 128), tiles, precision=HIGH
    )
    contrib = contrib * live[None, :, :, None]
    onehot = (col_ids[:, :, None] == jnp.arange(total)[None, None, :]).astype(jnp.float32)
    partial_grad = jnp.einsum("fbkc,bkj->fjc", contrib, onehot, precision=HIGH).reshape(
        width_part, total * 128
    )
    grad_feats = lax.psum_scatter(partial_grad, "node", scatter_dimension=1, tiled=True)
    return (out_t, grad_feats, grad_weight)


def solution(mesh):
    return jax.shard_map(
        on_device,
        mesh=mesh,
        in_specs=(
            P("feat", "node"),
            P(None, "feat"),
            P("feat", "node"),
            P("node", None, None, None),
            P("node", None),
            P("node"),
        ),
        out_specs=(P("feat", "node"), P("feat", "node"), P(None, "feat")),
        check_vma=False,
    )
```

profile of v0, /device:TPU:2, one launch (start us, length us, event | category | flops | bytes accessed | tf_op | source)
XLA Modules:
  0.0 1878.7 jit_solution(987238460676156024)
XLA Ops:
  9.5 1572.9 %while.16 = (s32[]{:T(128)}, f32[32,8,8,128]{3,0,2,1:T(8,128)S(1)}, s32[8,8]{1,0:T(8,128)S(1)}, s32[8,8]{1,0:T(8,128)S(1)}, f32[32,1024]{1,0:T(8,128)}, /*index=5*/s32[]{:T(128)}, u32[]{:T(128)}, u32[]{:T(128)}, s32[]{:T(128)}) while((s32[]{:T(128)}, f32[32,8,8,128]{3,0,2,1:T(8,128)S(1)}, s32[8,8]{1,0:T(8,128)S(1)}, ...), condition=%wide.region_2.3_spmd.clone, body=%wide.region_0.2_spmd.clone.sunk | while | flops 853639 | bytes 6298053 | solution.py:32
  10.4 98.7 %all-reduce.5.cloned.1.call-done = f32[32,8,128]{2,0,1:T(8,128)} async-done(((f32[32,8,128]{2,0,1:T(8,128)}), f32[32,8,128]{2,0,1:T(8,128)}) %all-reduce.5.cloned.1.call-update) | async-done | bytes 131088 | tf_op jit(solution)/shard_map/while/body/eval_jaxpr/psum | solution.py:11
  109.1 1.5 gather_fusion
  111.8 95.5 %all-reduce.5.cloned.1.call-done = f32[32,8,128]{2,0,1:T(8,128)} async-done(((f32[32,8,128]{2,0,1:T(8,128)}), f32[32,8,128]{2,0,1:T(8,128)}) %all-reduce.5.cloned.1.call-update) | async-done | bytes 131088 | tf_op jit(solution)/shard_map/while/body/eval_jaxpr/psum | solution.py:11
  207.4 1.5 gather_fusion
  210.1 95.5 %all-reduce.5.cloned.1.call-done = f32[32,8,128]{2,0,1:T(8,128)} async-done(((f32[32,8,128]{2,0,1:T(8,128)}), f32[32,8,128]{2,0,1:T(8,128)}) %all-reduce.5.cloned.1.call-update) | async-done | bytes 131088 | tf_op jit(solution)/shard_map/while/body/eval_jaxpr/psum | solution.py:11
  305.6 1.5 gather_fusion
  308.3 95.2 %all-reduce.5.cloned.1.call-done = f32[32,8,128]{2,0,1:T(8,128)} async-done(((f32[32,8,128]{2,0,1:T(8,128)}), f32[32,8,128]{2,0,1:T(8,128)}) %all-reduce.5.cloned.1.call-update) | async-done | bytes 131088 | tf_op jit(solution)/shard_map/while/body/eval_jaxpr/psum | solution.py:11
  403.6 1.5 gather_fusion
  405.5 1.6 copy_bitcast_fusion.4
  407.2 94.3 %all-reduce.5.cloned.1.call-done = f32[32,8,128]{2,0,1:T(8,128)} async-done(((f32[32,8,128]{2,0,1:T(8,128)}), f32[32,8,128]{2,0,1:T(8,128)}) %all-reduce.5.cloned.1.call-update) | async-done | bytes 131088 | tf_op jit(solution)/shard_map/while/body/eval_jaxpr/psum | solution.py:11
  501.5 1.5 gather_fusion
  504.2 95.2 %all-reduce.5.cloned.1.call-done = f32[32,8,128]{2,0,1:T(8,128)} async-done(((f32[32,8,128]{2,0,1:T(8,128)}), f32[32,8,128]{2,0,1:T(8,128)}) %all-reduce.5.cloned.1.call-update) | async-done | bytes 131088 | tf_op jit(solution)/shard_map/while/body/eval_jaxpr/psum | solution.py:11
  599.5 1.5 gather_fusion
  602.2 95.5 %all-reduce.5.cloned.1.call-done = f32[32,8,128]{2,0,1:T(8,128)} async-done(((f32[32,8,128]{2,0,1:T(8,128)}), f32[32,8,128]{2,0,1:T(8,128)}) %all-reduce.5.cloned.1.call-update) | async-done | bytes 131088 | tf_op jit(solution)/shard_map/while/body/eval_jaxpr/psum | solution.py:11
  697.7 1.5 gather_fusion
  700.5 95.5 %all-reduce.5.cloned.1.call-done = f32[32,8,128]{2,0,1:T(8,128)} async-done(((f32[32,8,128]{2,0,1:T(8,128)}), f32[32,8,128]{2,0,1:T(8,128)}) %all-reduce.5.cloned.1.call-update) | async-done | bytes 131088 | tf_op jit(solution)/shard_map/while/body/eval_jaxpr/psum | solution.py:11
  796.0 1.5 gather_fusion
  798.7 95.5 %all-reduce.5.cloned.1.call-done = f32[32,8,128]{2,0,1:T(8,128)} async-done(((f32[32,8,128]{2,0,1:T(8,128)}), f32[32,8,128]{2,0,1:T(8,128)}) %all-reduce.5.cloned.1.call-update) | async-done | bytes 131088 | tf_op jit(solution)/shard_map/while/body/eval_jaxpr/psum | solution.py:11
  894.2 1.5 gather_fusion
  897.0 95.2 %all-reduce.5.cloned.1.call-done = f32[32,8,128]{2,0,1:T(8,128)} async-done(((f32[32,8,128]{2,0,1:T(8,128)}), f32[32,8,128]{2,0,1:T(8,128)}) %all-reduce.5.cloned.1.call-update) | async-done | bytes 131088 | tf_op jit(solution)/shard_map/while/body/eval_jaxpr/psum | solution.py:11
  992.2 1.5 gather_fusion
  994.9 95.5 %all-reduce.5.cloned.1.call-done = f32[32,8,128]{2,0,1:T(8,128)} async-done(((f32[32,8,128]{2,0,1:T(8,128)}), f32[32,8,128]{2,0,1:T(8,128)}) %all-reduce.5.cloned.1.call-update) | async-done | bytes 131088 | tf_op jit(solution)/shard_map/while/body/eval_jaxpr/psum | solution.py:11
  1090.4 1.5 gather_fusion
  1093.2 95.2 %all-reduce.5.cloned.1.call-done = f32[32,8,128]{2,0,1:T(8,128)} async-done(((f32[32,8,128]{2,0,1:T(8,128)}), f32[32,8,128]{2,0,1:T(8,128)}) %all-reduce.5.cloned.1.call-update) | async-done | bytes 131088 | tf_op jit(solution)/shard_map/while/body/eval_jaxpr/psum | solution.py:11
  1188.4 1.5 gather_fusion
  1191.1 95.5 %all-reduce.5.cloned.1.call-done = f32[32,8,128]{2,0,1:T(8,128)} async-done(((f32[32,8,128]{2,0,1:T(8,128)}), f32[32,8,128]{2,0,1:T(8,128)}) %all-reduce.5.cloned.1.call-update) | async-done | bytes 131088 | tf_op jit(solution)/shard_map/while/body/eval_jaxpr/psum | solution.py:11
  1286.7 1.5 gather_fusion
  1289.4 95.2 %all-reduce.5.cloned.1.call-done = f32[32,8,128]{2,0,1:T(8,128)} async-done(((f32[32,8,128]{2,0,1:T(8,128)}), f32[32,8,128]{2,0,1:T(8,128)}) %all-reduce.5.cloned.1.call-update) | async-done | bytes 131088 | tf_op jit(solution)/shard_map/while/body/eval_jaxpr/psum | solution.py:11
  1384.6 1.5 gather_fusion
  1387.3 95.2 %all-reduce.5.cloned.1.call-done = f32[32,8,128]{2,0,1:T(8,128)} async-done(((f32[32,8,128]{2,0,1:T(8,128)}), f32[32,8,128]{2,0,1:T(8,128)}) %all-reduce.5.cloned.1.call-update) | async-done | bytes 131088 | tf_op jit(solution)/shard_map/while/body/eval_jaxpr/psum | solution.py:11
  1482.6 1.5 gather_fusion
  1485.3 95.2 %all-reduce.5.cloned.1.call-done = f32[32,8,128]{2,0,1:T(8,128)} async-done(((f32[32,8,128]{2,0,1:T(8,128)}), f32[32,8,128]{2,0,1:T(8,128)}) %all-reduce.5.cloned.1.call-update) | async-done | bytes 131088 | tf_op jit(solution)/shard_map/while/body/eval_jaxpr/psum | solution.py:11
  1580.5 1.5 gather_fusion
  1582.4 6.1 convolution_bitcast_fusion.1
  1589.3 39.5 %all-gather.2.cloned.1.call-done = f32[512,1024]{1,0:T(8,128)} async-done(((f32[32,1024]{1,0:T(8,128)}), f32[512,1024]{1,0:T(8,128)}) %all-gather.2.cloned.1.call-update) | async-done | bytes 2097168 | tf_op jit(solution)/shard_map/all_gather | solution.py:37
  1628.8 3.6 fusion.5
  1632.4 1.9 convolution_bitcast_fusion
  1634.3 1.8 copy.24
  1636.2 1.5 copy-done.1
  1637.7 2.7 fusion.12
  1640.5 53.4 %reduce-scatter.7.cloned.1.call-done = f32[32,1024]{1,0:T(8,128)} async-done(((f32[512,1024]{1,0:T(8,128)}), f32[32,1024]{1,0:T(8,128)}) %reduce-scatter.7.cloned.1.call-update) | async-done | bytes 131088
  1695.0 3.9 fusion
  1698.9 1.7 fusion.1
  1700.6 2.5 copy.34
  1703.2 83.2 %all-reduce.3.cloned.1.call-done = f32[512,32]{0,1:T(8,128)} async-done(((f32[512,32]{0,1:T(8,128)}), f32[512,32]{0,1:T(8,128)}) %all-reduce.3.cloned.1.call-update) | async-done | bytes 65552 | tf_op jit(solution)/shard_map/psum | solution.py:42
  1786.4 83.4 %reduce-scatter.5.cloned.1.call-done = f32[32,1024]{1,0:T(8,128)} async-done(((f32[32,16384]{1,0:T(8,128)}), f32[32,1024]{1,0:T(8,128)}) %reduce-scatter.5.cloned.1.call-update) | async-done | bytes 131088 | tf_op jit(solution)/shard_map/reduce_scatter | solution.py:54
  1869.8 1.5 copy.46
  (147 shorter events, 21.0 us)
Async XLA Ops:
  8.0 1620.8 %copy-start = (f32[512,32]{0,1:T(8,128)S(1)}, f32[512,32]{0,1:T(8,128)}, u32[]{:S(2)}) copy-start(f32[512,32]{0,1:T(8,128)} %param.9) | copy-start | bytes 196612
  9.5 99.6 %all-reduce.5.cloned.1.call-start = ((), (), s32[]{:S(2)}) async-start(), calls=%async_computation.6 | async-start | bytes 262144 | tf_op jit(solution)/shard_map/while/body/eval_jaxpr/psum | solution.py:11
  110.9 96.4 %all-reduce.5.cloned.1.call-start = ((), (), s32[]{:S(2)}) async-start(), calls=%async_computation.6 | async-start | bytes 262144 | tf_op jit(solution)/shard_map/while/body/eval_jaxpr/psum | solution.py:11
  209.2 96.4 %all-reduce.5.cloned.1.call-start = ((), (), s32[]{:S(2)}) async-start(), calls=%async_computation.6 | async-start | bytes 262144 | tf_op jit(solution)/shard_map/while/body/eval_jaxpr/psum | solution.py:11
  307.4 96.1 %all-reduce.5.cloned.1.call-start = ((), (), s32[]{:S(2)}) async-start(), calls=%async_computation.6 | async-start | bytes 262144 | tf_op jit(solution)/shard_map/while/body/eval_jaxpr/psum | solution.py:11
  405.4 96.1 %all-reduce.5.cloned.1.call-start = ((), (), s32[]{:S(2)}) async-start(), calls=%async_computation.6 | async-start | bytes 262144 | tf_op jit(solution)/shard_map/while/body/eval_jaxpr/psum | solution.py:11
  503.4 96.1 %all-reduce.5.cloned.1.call-start = ((), (), s32[]{:S(2)}) async-start(), calls=%async_computation.6 | async-start | bytes 262144 | tf_op jit(solution)/shard_map/while/body/eval_jaxpr/psum | solution.py:11
  601.3 96.4 %all-reduce.5.cloned.1.call-start = ((), (), s32[]{:S(2)}) async-start(), calls=%async_computation.6 | async-start | bytes 262144 | tf_op jit(solution)/shard_map/while/body/eval_jaxpr/psum | solution.py:11
  699.6 96.4 %all-reduce.5.cloned.1.call-start = ((), (), s32[]{:S(2)}) async-start(), calls=%async_computation.6 | async-start | bytes 262144 | tf_op jit(solution)/shard_map/while/body/eval_jaxpr/psum | solution.py:11
  797.8 96.4 %all-reduce.5.cloned.1.call-start = ((), (), s32[]{:S(2)}) async-start(), calls=%async_computation.6 | async-start | bytes 262144 | tf_op jit(solution)/shard_map/while/body/eval_jaxpr/psum | solution.py:11
  896.1 96.1 %all-reduce.5.cloned.1.call-start = ((), (), s32[]{:S(2)}) async-start(), calls=%async_computation.6 | async-start | bytes 262144 | tf_op jit(solution)/shard_map/while/body/eval_jaxpr/psum | solution.py:11
  994.0 96.4 %all-reduce.5.cloned.1.call-start = ((), (), s32[]{:S(2)}) async-start(), calls=%async_computation.6 | async-start | bytes 262144 | tf_op jit(solution)/shard_map/while/body/eval_jaxpr/psum | solution.py:11
  1092.3 96.1 %all-reduce.5.cloned.1.call-start = ((), (), s32[]{:S(2)}) async-start(), calls=%async_computation.6 | async-start | bytes 262144 | tf_op jit(solution)/shard_map/while/body/eval_jaxpr/psum | solution.py:11
  1190.2 96.4 %all-reduce.5.cloned.1.call-start = ((), (), s32[]{:S(2)}) async-start(), calls=%async_computation.6 | async-start | bytes 262144 | tf_op jit(solution)/shard_map/while/body/eval_jaxpr/psum | solution.py:11
  1288.5 96.1 %all-reduce.5.cloned.1.call-start = ((), (), s32[]{:S(2)}) async-start(), calls=%async_computation.6 | async-start | bytes 262144 | tf_op jit(solution)/shard_map/while/body/eval_jaxpr/psum | solution.py:11
  1386.5 96.1 %all-reduce.5.cloned.1.call-start = ((), (), s32[]{:S(2)}) async-start(), calls=%async_computation.6 | async-start | bytes 262144 | tf_op jit(solution)/shard_map/while/body/eval_jaxpr/psum | solution.py:11
  1484.4 96.1 %all-reduce.5.cloned.1.call-start = ((), (), s32[]{:S(2)}) async-start(), calls=%async_computation.6 | async-start | bytes 262144 | tf_op jit(solution)/shard_map/while/body/eval_jaxpr/psum | solution.py:11
  1582.4 46.4 %all-gather.2.cloned.1.call-start = ((), (), s32[]{:S(2)}) async-start(), calls=%async_computation.2 | async-start | bytes 2228224 | tf_op jit(solution)/shard_map/all_gather | solution.py:37
  1588.5 43.9 %copy-start.2 = (f32[32,1024]{1,0:T(8,128)S(1)}, f32[32,1024]{1,0:T(8,128)}, u32[]{:S(2)}) copy-start(f32[32,1024]{1,0:T(8,128)} %param.10) | copy-start | bytes 393220
  1589.2 104.7 %reduce-scatter.7.cloned.1.call-start = ((), (), s32[]{:S(2)}) async-start(), calls=%async_computation.5 | async-start | bytes 2228224
  1636.1 1.6 copy-start.1
  1636.1 150.3 %all-reduce.3.cloned.1.call-start = ((), (), s32[]{:S(2)}) async-start(), calls=%async_computation.4 | async-start | bytes 131072 | tf_op jit(solution)/shard_map/psum | solution.py:42
  1640.4 229.4 %reduce-scatter.5.cloned.1.call-start = ((), (), s32[]{:S(2)}) async-start(), calls=%async_computation.3 | async-start | bytes 2228224 | tf_op jit(solution)/shard_map/reduce_scatter | solution.py:54
  1695.0 3.9 copy-start.3
Sparse Core Ops, SparseCore 0:
  14.1 94.9 all-reduce.4
  115.6 91.7 all-reduce.4
  213.8 91.7 all-reduce.4
  311.7 91.7 all-reduce.4
  409.7 91.7 all-reduce.4
  507.7 91.7 all-reduce.4
  605.9 91.7 all-reduce.4
  704.2 91.7 all-reduce.4
  802.4 91.7 all-reduce.4
  900.4 91.7 all-reduce.4
  998.6 91.7 all-reduce.4
  1096.6 91.7 all-reduce.4
  1194.9 91.7 all-reduce.4
  1292.8 91.7 all-reduce.4
  1390.8 91.7 all-reduce.4
  1488.7 91.7 all-reduce.4
Sparse Core Ops, SparseCore 1:
  1589.3 39.4 all-gather.1
  1636.2 57.6 reduce-scatter.6
  1697.5 88.9 all-reduce.2
  1791.0 78.8 reduce-scatter.4
where the time goes:
time: 1880 us
  waiting for transfers between devices  1790 us (95%)
  local copies, waits for them, and re-layouts  34.7 us (2%)
  matrix products  19.9 us (1%)
    psum x16, waiting for transfers between devices, from_root(): return lax.psum(kept, axis)  1530 us
    reduce_scatter x1, waiting for transfers between devices, on_device(): lax.psum_scatter(partial_grad, 'node', scatter_dimension=1, tiled=True)  83.4 us
    psum x1, waiting for transfers between devices, on_device(): lax.psum(jnp.dot(mixed_full, grad_pre.T, precision=HIGH), 'node')  83.2 us
    unnamed x5, waiting for transfers between devices  53.5 us
    all_gather x1, waiting for transfers between devices, on_device(): mixed_full = lax.all_gather(mixed_t, 'feat', axis=0, tiled=True)  39.5 us
  transfers between devices with their start and end apart: 20, of which 20 were waited for; matrix products, arithmetic and copies ran while one was open for 1% of the time, Pallas kernels for 0%

commit v1 on v0

--- a/solution.py
+++ b/solution.py
@@ -34,7 +34,9 @@
     mixed_t = jnp.einsum("fbkc,bkrc->fbr", selected, tiles, precision=HIGH).reshape(
         width_part, rows
     )
-    mixed_full = lax.all_gather(mixed_t, "feat", axis=0, tiled=True)
+    mixed_full = jnp.concatenate(
+        lax.all_to_all(jnp.stack([mixed_t] * lax.axis_size("feat")), "feat", 0, 0), axis=0
+    )
     pre_t = jnp.dot(weight.T, mixed_full, precision=HIGH)
     sig = jax.nn.sigmoid(pre_t)
     out_t = pre_t * sig

time: 1880 us -> 1840 us (0.979)
  waiting for transfers between devices: 1790 us -> 1690 us
  blocking collectives: 0 us -> 56.7 us
    psum x1, waiting for transfers between devices: 83.2 us -> 26.2 us  [on_device(): lax.psum(jnp.dot(mixed_full, grad_pre.T, precision=HIGH), 'node')]
    all_to_all x0 -> x1, blocking collectives: none -> 56.7 us  [on_device(): lax.all_to_all(jnp.stack([mixed_t] * lax.axis_size('feat')), 'feat', 0, 0)]
    all_gather x1 -> x0, waiting for transfers between devices: 39.5 us -> none  [on_device(): mixed_full = lax.all_gather(mixed_t, 'feat', axis=0, tiled=True)]
    unnamed x5 -> x4, waiting for transfers between devices: 53.5 us -> 53.6 us
  transfers between devices with their start and end apart: 20 -> 19, of which waited for: 20 -> 19; matrix products, arithmetic and copies ran while one was open for 1% -> 1% of each run, Pallas kernels for 0% -> 0%
where the time goes in v1:
time: 1840 us
  waiting for transfers between devices  1690 us (92%)
  blocking collectives  56.7 us (3%)
  local copies, waits for them, and re-layouts  33.9 us (2%)
  matrix products  19.6 us (1%)
    psum x16, waiting for transfers between devices, from_root(): return lax.psum(kept, axis)  1530 us
    reduce_scatter x1, waiting for transfers between devices, on_device(): lax.psum_scatter(partial_grad, 'node', scatter_dimension=1, tiled=True)  83.2 us
    all_to_all x1, blocking collectives, on_device(): lax.all_to_all(jnp.stack([mixed_t] * lax.axis_size('feat')), 'feat', 0, 0)  56.7 us
    unnamed x4, waiting for transfers between devices  53.6 us
  transfers between devices with their start and end apart: 19, of which 19 were waited for; matrix products, arithmetic and copies ran while one was open for 1% of the time, Pallas kernels for 0%

profile of v1, /device:TPU:2, one launch (start us, length us, event | category | flops | bytes accessed | tf_op | source)
XLA Modules:
  0.0 1837.6 jit_solution(15740148400103368353)
XLA Ops:
  9.5 1572.9 %while.16 = (s32[]{:T(128)}, f32[32,8,8,128]{3,0,2,1:T(8,128)S(1)}, s32[8,8]{1,0:T(8,128)S(1)}, s32[8,8]{1,0:T(8,128)S(1)}, f32[32,1024]{1,0:T(8,128)}, /*index=5*/s32[]{:T(128)}, u32[]{:T(128)}, u32[]{:T(128)}, s32[]{:T(128)}) while((s32[]{:T(128)}, f32[32,8,8,128]{3,0,2,1:T(8,128)S(1)}, s32[8,8]{1,0:T(8,128)S(1)}, ...), condition=%wide.region_2.3_spmd.clone, body=%wide.region_0.2_spmd.clone.sunk | while | flops 853639 | bytes 6298053 | solution.py:32
  10.4 98.7 %all-reduce.5.cloned.1.call-done = f32[32,8,128]{2,0,1:T(8,128)} async-done(((f32[32,8,128]{2,0,1:T(8,128)}), f32[32,8,128]{2,0,1:T(8,128)}) %all-reduce.5.cloned.1.call-update) | async-done | bytes 131088 | tf_op jit(solution)/shard_map/while/body/eval_jaxpr/psum | solution.py:11
  109.1 1.5 gather_fusion
  111.8 95.5 %all-reduce.5.cloned.1.call-done = f32[32,8,128]{2,0,1:T(8,128)} async-done(((f32[32,8,128]{2,0,1:T(8,128)}), f32[32,8,128]{2,0,1:T(8,128)}) %all-reduce.5.cloned.1.call-update) | async-done | bytes 131088 | tf_op jit(solution)/shard_map/while/body/eval_jaxpr/psum | solution.py:11
  207.4 1.5 gather_fusion
  210.1 95.5 %all-reduce.5.cloned.1.call-done = f32[32,8,128]{2,0,1:T(8,128)} async-done(((f32[32,8,128]{2,0,1:T(8,128)}), f32[32,8,128]{2,0,1:T(8,128)}) %all-reduce.5.cloned.1.call-update) | async-done | bytes 131088 | tf_op jit(solution)/shard_map/while/body/eval_jaxpr/psum | solution.py:11
  305.6 1.5 gather_fusion
  308.3 95.2 %all-reduce.5.cloned.1.call-done = f32[32,8,128]{2,0,1:T(8,128)} async-done(((f32[32,8,128]{2,0,1:T(8,128)}), f32[32,8,128]{2,0,1:T(8,128)}) %all-reduce.5.cloned.1.call-update) | async-done | bytes 131088 | tf_op jit(solution)/shard_map/while/body/eval_jaxpr/psum | solution.py:11
  403.6 1.5 gather_fusion
  405.5 1.6 copy_bitcast_fusion.4
  407.2 94.3 %all-reduce.5.cloned.1.call-done = f32[32,8,128]{2,0,1:T(8,128)} async-done(((f32[32,8,128]{2,0,1:T(8,128)}), f32[32,8,128]{2,0,1:T(8,128)}) %all-reduce.5.cloned.1.call-update) | async-done | bytes 131088 | tf_op jit(solution)/shard_map/while/body/eval_jaxpr/psum | solution.py:11
  501.5 1.5 gather_fusion
  504.2 95.2 %all-reduce.5.cloned.1.call-done = f32[32,8,128]{2,0,1:T(8,128)} async-done(((f32[32,8,128]{2,0,1:T(8,128)}), f32[32,8,128]{2,0,1:T(8,128)}) %all-reduce.5.cloned.1.call-update) | async-done | bytes 131088 | tf_op jit(solution)/shard_map/while/body/eval_jaxpr/psum | solution.py:11
  599.5 1.5 gather_fusion
  602.2 95.5 %all-reduce.5.cloned.1.call-done = f32[32,8,128]{2,0,1:T(8,128)} async-done(((f32[32,8,128]{2,0,1:T(8,128)}), f32[32,8,128]{2,0,1:T(8,128)}) %all-reduce.5.cloned.1.call-update) | async-done | bytes 131088 | tf_op jit(solution)/shard_map/while/body/eval_jaxpr/psum | solution.py:11
  697.7 1.5 gather_fusion
  700.5 95.5 %all-reduce.5.cloned.1.call-done = f32[32,8,128]{2,0,1:T(8,128)} async-done(((f32[32,8,128]{2,0,1:T(8,128)}), f32[32,8,128]{2,0,1:T(8,128)}) %all-reduce.5.cloned.1.call-update) | async-done | bytes 131088 | tf_op jit(solution)/shard_map/while/body/eval_jaxpr/psum | solution.py:11
  796.0 1.5 gather_fusion
  798.7 95.5 %all-reduce.5.cloned.1.call-done = f32[32,8,128]{2,0,1:T(8,128)} async-done(((f32[32,8,128]{2,0,1:T(8,128)}), f32[32,8,128]{2,0,1:T(8,128)}) %all-reduce.5.cloned.1.call-update) | async-done | bytes 131088 | tf_op jit(solution)/shard_map/while/body/eval_jaxpr/psum | solution.py:11
  894.2 1.5 gather_fusion
  897.0 95.2 %all-reduce.5.cloned.1.call-done = f32[32,8,128]{2,0,1:T(8,128)} async-done(((f32[32,8,128]{2,0,1:T(8,128)}), f32[32,8,128]{2,0,1:T(8,128)}) %all-reduce.5.cloned.1.call-update) | async-done | bytes 131088 | tf_op jit(solution)/shard_map/while/body/eval_jaxpr/psum | solution.py:11
  992.2 1.5 gather_fusion
  994.9 95.5 %all-reduce.5.cloned.1.call-done = f32[32,8,128]{2,0,1:T(8,128)} async-done(((f32[32,8,128]{2,0,1:T(8,128)}), f32[32,8,128]{2,0,1:T(8,128)}) %all-reduce.5.cloned.1.call-update) | async-done | bytes 131088 | tf_op jit(solution)/shard_map/while/body/eval_jaxpr/psum | solution.py:11
  1090.4 1.5 gather_fusion
  1093.2 95.2 %all-reduce.5.cloned.1.call-done = f32[32,8,128]{2,0,1:T(8,128)} async-done(((f32[32,8,128]{2,0,1:T(8,128)}), f32[32,8,128]{2,0,1:T(8,128)}) %all-reduce.5.cloned.1.call-update) | async-done | bytes 131088 | tf_op jit(solution)/shard_map/while/body/eval_jaxpr/psum | solution.py:11
  1188.4 1.5 gather_fusion
  1191.1 95.5 %all-reduce.5.cloned.1.call-done = f32[32,8,128]{2,0,1:T(8,128)} async-done(((f32[32,8,128]{2,0,1:T(8,128)}), f32[32,8,128]{2,0,1:T(8,128)}) %all-reduce.5.cloned.1.call-update) | async-done | bytes 131088 | tf_op jit(solution)/shard_map/while/body/eval_jaxpr/psum | solution.py:11
  1286.7 1.5 gather_fusion
  1289.4 95.2 %all-reduce.5.cloned.1.call-done = f32[32,8,128]{2,0,1:T(8,128)} async-done(((f32[32,8,128]{2,0,1:T(8,128)}), f32[32,8,128]{2,0,1:T(8,128)}) %all-reduce.5.cloned.1.call-update) | async-done | bytes 131088 | tf_op jit(solution)/shard_map/while/body/eval_jaxpr/psum | solution.py:11
  1384.6 1.5 gather_fusion
  1387.3 95.2 %all-reduce.5.cloned.1.call-done = f32[32,8,128]{2,0,1:T(8,128)} async-done(((f32[32,8,128]{2,0,1:T(8,128)}), f32[32,8,128]{2,0,1:T(8,128)}) %all-reduce.5.cloned.1.call-update) | async-done | bytes 131088 | tf_op jit(solution)/shard_map/while/body/eval_jaxpr/psum | solution.py:11
  1482.6 1.5 gather_fusion
  1485.3 95.2 %all-reduce.5.cloned.1.call-done = f32[32,8,128]{2,0,1:T(8,128)} async-done(((f32[32,8,128]{2,0,1:T(8,128)}), f32[32,8,128]{2,0,1:T(8,128)}) %all-reduce.5.cloned.1.call-update) | async-done | bytes 131088 | tf_op jit(solution)/shard_map/while/body/eval_jaxpr/psum | solution.py:11
  1580.5 1.5 gather_fusion
  1582.4 6.1 convolution_bitcast_fusion.1
  1588.8 56.7 %all_to_all.5 = f32[16,32,1024]{2,1,0:T(8,128)S(1)} all-to-all(f32[16,32,1024]{2,1,0:T(8,128)S(1)} %stack.3), channel_id=1, replica_groups=mesh['node'=16,'feat'=16] {'feat'}, dimensions={0} | all-to-all | bytes 4194304 | tf_op jit(solution)/shard_map/all_to_all | solution.py:38
  1645.4 2.0 fusion.5
  1647.5 3.2 convolution_bitcast_fusion
  1650.6 2.9 copy.24
  1653.7 2.7 fusion.12
  1656.5 53.5 %reduce-scatter.7.cloned.1.call-done = f32[32,1024]{1,0:T(8,128)} async-done(((f32[512,1024]{1,0:T(8,128)}), f32[32,1024]{1,0:T(8,128)}) %reduce-scatter.7.cloned.1.call-update) | async-done | bytes 131088
  1710.0 1.1 copy.25
  1711.1 3.9 fusion
  1715.1 1.7 fusion.1
  1716.8 2.6 copy.34
  1719.3 26.2 %all-reduce.3.cloned.1.call-done = f32[512,32]{0,1:T(8,128)} async-done(((f32[512,32]{0,1:T(8,128)}), f32[512,32]{0,1:T(8,128)}) %all-reduce.3.cloned.1.call-update) | async-done | bytes 65552 | tf_op jit(solution)/shard_map/psum | solution.py:44
  1745.5 83.2 %reduce-scatter.5.cloned.1.call-done = f32[32,1024]{1,0:T(8,128)} async-done(((f32[32,16384]{1,0:T(8,128)}), f32[32,1024]{1,0:T(8,128)}) %reduce-scatter.5.cloned.1.call-update) | async-done | bytes 131088 | tf_op jit(solution)/shard_map/reduce_scatter | solution.py:56
  1828.7 1.5 copy.46
  (144 shorter events, 19.4 us)
Async XLA Ops:
  8.0 1637.4 %copy-start = (f32[512,32]{0,1:T(8,128)S(1)}, f32[512,32]{0,1:T(8,128)}, u32[]{:S(2)}) copy-start(f32[512,32]{0,1:T(8,128)} %param.9) | copy-start | bytes 196612
  9.5 99.6 %all-reduce.5.cloned.1.call-start = ((), (), s32[]{:S(2)}) async-start(), calls=%async_computation.6 | async-start | bytes 262144 | tf_op jit(solution)/shard_map/while/body/eval_jaxpr/psum | solution.py:11
  110.9 96.4 %all-reduce.5.cloned.1.call-start = ((), (), s32[]{:S(2)}) async-start(), calls=%async_computation.6 | async-start | bytes 262144 | tf_op jit(solution)/shard_map/while/body/eval_jaxpr/psum | solution.py:11
  209.2 96.4 %all-reduce.5.cloned.1.call-start = ((), (), s32[]{:S(2)}) async-start(), calls=%async_computation.6 | async-start | bytes 262144 | tf_op jit(solution)/shard_map/while/body/eval_jaxpr/psum | solution.py:11
  307.4 96.1 %all-reduce.5.cloned.1.call-start = ((), (), s32[]{:S(2)}) async-start(), calls=%async_computation.6 | async-start | bytes 262144 | tf_op jit(solution)/shard_map/while/body/eval_jaxpr/psum | solution.py:11
  405.4 96.1 %all-reduce.5.cloned.1.call-start = ((), (), s32[]{:S(2)}) async-start(), calls=%async_computation.6 | async-start | bytes 262144 | tf_op jit(solution)/shard_map/while/body/eval_jaxpr/psum | solution.py:11
  503.4 96.1 %all-reduce.5.cloned.1.call-start = ((), (), s32[]{:S(2)}) async-start(), calls=%async_computation.6 | async-start | bytes 262144 | tf_op jit(solution)/shard_map/while/body/eval_jaxpr/psum | solution.py:11
  601.3 96.4 %all-reduce.5.cloned.1.call-start = ((), (), s32[]{:S(2)}) async-start(), calls=%async_computation.6 | async-start | bytes 262144 | tf_op jit(solution)/shard_map/while/body/eval_jaxpr/psum | solution.py:11
  699.6 96.4 %all-reduce.5.cloned.1.call-start = ((), (), s32[]{:S(2)}) async-start(), calls=%async_computation.6 | async-start | bytes 262144 | tf_op jit(solution)/shard_map/while/body/eval_jaxpr/psum | solution.py:11
  797.8 96.4 %all-reduce.5.cloned.1.call-start = ((), (), s32[]{:S(2)}) async-start(), calls=%async_computation.6 | async-start | bytes 262144 | tf_op jit(solution)/shard_map/while/body/eval_jaxpr/psum | solution.py:11
  896.1 96.1 %all-reduce.5.cloned.1.call-start = ((), (), s32[]{:S(2)}) async-start(), calls=%async_computation.6 | async-start | bytes 262144 | tf_op jit(solution)/shard_map/while/body/eval_jaxpr/psum | solution.py:11
  994.0 96.4 %all-reduce.5.cloned.1.call-start = ((), (), s32[]{:S(2)}) async-start(), calls=%async_computation.6 | async-start | bytes 262144 | tf_op jit(solution)/shard_map/while/body/eval_jaxpr/psum | solution.py:11
  1092.3 96.1 %all-reduce.5.cloned.1.call-start = ((), (), s32[]{:S(2)}) async-start(), calls=%async_computation.6 | async-start | bytes 262144 | tf_op jit(solution)/shard_map/while/body/eval_jaxpr/psum | solution.py:11
  1190.2 96.4 %all-reduce.5.cloned.1.call-start = ((), (), s32[]{:S(2)}) async-start(), calls=%async_computation.6 | async-start | bytes 262144 | tf_op jit(solution)/shard_map/while/body/eval_jaxpr/psum | solution.py:11
  1288.5 96.1 %all-reduce.5.cloned.1.call-start = ((), (), s32[]{:S(2)}) async-start(), calls=%async_computation.6 | async-start | bytes 262144 | tf_op jit(solution)/shard_map/while/body/eval_jaxpr/psum | solution.py:11
  1386.5 96.1 %all-reduce.5.cloned.1.call-start = ((), (), s32[]{:S(2)}) async-start(), calls=%async_computation.6 | async-start | bytes 262144 | tf_op jit(solution)/shard_map/while/body/eval_jaxpr/psum | solution.py:11
  1484.4 96.1 %all-reduce.5.cloned.1.call-start = ((), (), s32[]{:S(2)}) async-start(), calls=%async_computation.6 | async-start | bytes 262144 | tf_op jit(solution)/shard_map/while/body/eval_jaxpr/psum | solution.py:11
  1582.4 127.6 %reduce-scatter.7.cloned.1.call-start = ((), (), s32[]{:S(2)}) async-start(), calls=%async_computation.5 | async-start | bytes 2228224
  1645.4 2.0 copy-start.1
  1653.6 91.9 %all-reduce.3.cloned.1.call-start = ((), (), s32[]{:S(2)}) async-start(), calls=%async_computation.4 | async-start | bytes 131072 | tf_op jit(solution)/shard_map/psum | solution.py:44
  1656.4 172.3 %reduce-scatter.5.cloned.1.call-start = ((), (), s32[]{:S(2)}) async-start(), calls=%async_computation.3 | async-start | bytes 2228224 | tf_op jit(solution)/shard_map/reduce_scatter | solution.py:56
  1711.1 3.9 copy-start.2
Sparse Core Ops, SparseCore 0:
  14.1 94.9 all-reduce.4
  115.6 91.7 all-reduce.4
  213.8 91.7 all-reduce.4
  311.7 91.7 all-reduce.4
  409.7 91.7 all-reduce.4
  507.7 91.7 all-reduce.4
  605.9 91.7 all-reduce.4
  704.2 91.7 all-reduce.4
  802.4 91.7 all-reduce.4
  900.4 91.7 all-reduce.4
  998.6 91.7 all-reduce.4
  1096.6 91.7 all-reduce.4
  1194.9 91.7 all-reduce.4
  1292.8 91.7 all-reduce.4
  1390.8 91.7 all-reduce.4
  1488.7 91.7 all-reduce.4
  1657.9 87.5 all-reduce.2
  1749.9 78.7 reduce-scatter.4
Sparse Core Ops, SparseCore 1:
  1653.7 56.2 reduce-scatter.6
